TPU v7x, 512 devices: a whole 4x4x16 slice. The times are simulated.
512 devices in a mesh: row: 32 (over z, core), col: 16 (over x, y).
Axes of the slice: x: 4, y: 4, z: 16, core: 2. Of those that a mesh axis runs over, the one named last changes fastest.
Arguments:
- factor: bfloat16 [2, 32, 4, 16, 256, 256], P(None, 'row', None, 'col'), may hold values from -0.0625 to 0.0625
- pattern: int32 [2, 32, 4, 16], P(None, 'row', None, 'col'), may hold values from 0 to 1
- dinv: bfloat16 [2, 32, 256, 256], P(None, 'row'), may hold values from -3 to 3
- rhs: float32 [2, 32, 256, 256], P(None, 'row'), may hold values from -6 to 6
Outputs:
- forward: bfloat16 [2, 32, 256, 256], P(None, 'row')
- solution: bfloat16 [2, 32, 256, 256], P(None, 'row')
All inputs are finite; a program needn't handle non-finite values.
Results may differ from a plain program's by a relative error of at most 0.0075.
Values may be sent and summed in bfloat16 or wider, within the bound.
A program may use at most 64 MiB of HBM per device.

v0:
```python
import jax
import jax.numpy as jnp
from jax import lax
from jax.sharding import PartitionSpec as P


def broadcast(value, axis, root):
    mine = lax.axis_index(axis) == root
    return lax.psum(jnp.where(mine, value, jnp.zeros_like(value)), axis)


def per_device(factor, pattern, dinv, rhs):
    n_row = lax.axis_size("row")
    n_col = lax.axis_size("col")
    row_idx = lax.axis_index("row")
    col_idx = lax.axis_index("col")
    kr_local = factor.shape[0]
    levels = factor.shape[2]
    size_b = factor.shape[4]
    size_r = rhs.shape[3]
    upper_limit = lax.Precision.HIGHEST
    blocks = factor[:, 0, :, 0]
    row_level = (jnp.arange(kr_local, dtype=jnp.int32) * n_row + row_idx) // n_col
    allowed = (row_level[:, None] > jnp.arange(levels, dtype=jnp.int32)[None, :]).astype(jnp.int32)
    weights = (pattern[:, 0, :, 0] * allowed).astype(jnp.float32)
    inverse_blocks = dinv[:, 0].astype(jnp.float32)
    right_side = rhs[:, 0]
    half_idx = row_idx // n_col
    empty = jnp.zeros((size_b, size_r), jnp.bfloat16)
    pending = jnp.zeros((kr_local, size_b, size_r), jnp.float32)
    forward_rows = [empty for step in range(kr_local)]
    for m in range(levels):
        slot = m // 2
        active = half_idx == m % 2
        if m == 0:
            total = jnp.zeros((size_b, size_r), jnp.float32)
        else:
            total = lax.psum(pending[slot], "col")
        solved = jnp.dot(
            inverse_blocks[slot], right_side[slot] - total, precision=upper_limit
        ).astype(jnp.bfloat16)
        forward_rows[slot] = jnp.where(active, solved, forward_rows[slot])
        if m + 1 < levels:
            root = (m * n_col + col_idx) % n_row
            panel = broadcast(solved, "row", root)
            update = jnp.einsum(
                "abc,cr->abr", blocks[slot:, m], panel, preferred_element_type=jnp.float32
            )
            pending = pending.at[slot:].add(weights[slot:, m][:, None, None] * update)
    backlog = jnp.zeros((levels, size_b, size_r), jnp.float32)
    solution_rows = [empty for step in range(kr_local)]
    root_col = row_idx % n_col
    for m in range(levels - 1, -1, -1):
        slot = m // 2
        active = half_idx == m % 2
        if m == levels - 1:
            total = jnp.zeros((size_b, size_r), jnp.float32)
        else:
            total = lax.psum(backlog[m], "row")
        residue = forward_rows[slot].astype(jnp.float32) - total
        solved = jnp.dot(inverse_blocks[slot].T, residue, precision=upper_limit).astype(
            jnp.bfloat16
        )
        received = broadcast(solved, "col", root_col)
        received = jnp.where(active, received, empty)
        solution_rows[slot] = jnp.where(active, received, solution_rows[slot])
        if m > 0:
            update = jnp.einsum(
                "bij,ir->bjr", blocks[slot, :m], received, preferred_element_type=jnp.float32
            )
            backlog = backlog.at[:m].add(weights[slot, :m][:, None, None] * update)
    forward = jnp.stack(forward_rows)[:, None]
    solution = jnp.stack(solution_rows)[:, None]
    return (forward, solution)


def solution(mesh):
    placed = (
        P(None, "row", None, "col", None, None),
        P(None, "row", None, "col"),
        P(None, "row", None, None),
        P(None, "row", None, None),
    )
    return jax.shard_map(
        per_device,
        mesh=mesh,
        in_specs=placed,
        out_specs=(P(None, "row", None, None), P(None, "row", None, None)),
        check_vma=False,
    )
```

profile of v0, /device:TPU:1, one launch (start us, length us, event | category | flops | bytes accessed | tf_op | source)
XLA Modules:
  0.0 2050.8 jit_solution(6329169236975425313)
XLA Ops:
  7.2 0.0 all-reduce.14.cloned.1.call-start
  7.2 1.4 convolution_convert_fusion.6
  8.6 0.1 copy.26
  8.8 0.7 broadcast_select_fusion.2
  9.4 0.0 all-reduce.14.cloned.1.call-update
  9.5 0.0 all-reduce.16.cloned.1.call-start
  9.5 0.1 copy.52
  9.6 0.7 copy-done.6
  10.3 0.1 fusion.49
  10.4 0.2 slice_reduce_fusion.1
  10.5 201.5 %all-reduce.14.cloned.1.call-done = bf16[256,256]{0,1:T(8,128)(2,1)} async-done(((bf16[256,256]{0,1:T(8,128)(2,1)}), bf16[256,256]{0,1:T(8,128)(2,1)}) %all-reduce.14.cloned.1.call-update) | async-done | bytes 131088 | tf_op jit(solution)/shard_map/psum | solution.py:9
  212.1 1.2 fusion.4
  213.2 0.7 slice_bitcast_fusion.8
  214.0 0.0 all-reduce.16.cloned.1.call-update
  214.0 0.0 all-reduce.18.cloned.1.call-start
  214.1 0.3 copy-done.1
  214.4 0.1 copy.49
  214.6 111.0 %all-reduce.16.cloned.1.call-done = f32[256,256]{0,1:T(8,128)} async-done(((f32[256,256]{0,1:T(8,128)}), f32[256,256]{0,1:T(8,128)}) %all-reduce.16.cloned.1.call-update) | async-done | bytes 262160 | tf_op jit(solution)/shard_map/psum | solution.py:38
  325.6 2.0 broadcast_select_fusion
  327.6 0.0 all-reduce.20.cloned.1.call-start
  327.6 197.5 %all-reduce.18.cloned.1.call-done = bf16[256,256]{0,1:T(8,128)(2,1)} async-done(((bf16[256,256]{0,1:T(8,128)(2,1)}), bf16[256,256]{0,1:T(8,128)(2,1)}) %all-reduce.18.cloned.1.call-update) | async-done | bytes 131088 | tf_op jit(solution)/shard_map/psum | solution.py:9
  525.1 1.2 fusion.3
  526.3 0.7 fusion.37
  527.0 0.0 all-reduce.20.cloned.1.call-update
  527.0 0.0 all-reduce.22.cloned.1.call-start
  527.1 0.1 copy.50
  527.3 111.2 %all-reduce.20.cloned.1.call-done = f32[256,256]{0,1:T(8,128)} async-done(((f32[256,256]{0,1:T(8,128)}), f32[256,256]{0,1:T(8,128)}) %all-reduce.20.cloned.1.call-update) | async-done | bytes 262160 | tf_op jit(solution)/shard_map/psum | solution.py:38
  638.5 1.3 convolution_convert_fusion.4
  639.8 0.7 select_bitcast_fusion.2
  640.4 0.0 all-reduce.22.cloned.1.call-update
  640.5 0.0 all-reduce.24.cloned.1.call-start
  640.5 0.6 fusion.55
  641.1 196.8 %all-reduce.22.cloned.1.call-done = bf16[256,256]{1,0:T(8,128)(2,1)} async-done(((bf16[256,256]{1,0:T(8,128)(2,1)}), bf16[256,256]{1,0:T(8,128)(2,1)}) %all-reduce.22.cloned.1.call-update) | async-done | bytes 131088 | tf_op jit(solution)/shard_map/psum | solution.py:9
  837.9 2.4 fusion.8
  840.3 0.0 all-reduce.26.cloned.1.call-start
  840.4 110.9 %all-reduce.24.cloned.1.call-done = f32[256,256]{0,1:T(8,128)} async-done(((f32[256,256]{0,1:T(8,128)}), f32[256,256]{0,1:T(8,128)}) %all-reduce.24.cloned.1.call-update) | async-done | bytes 262160 | tf_op jit(solution)/shard_map/psum | solution.py:38
  951.2 1.3 fusion.12
  952.5 0.9 fusion.20
  953.4 0.0 all-reduce.28.cloned.1.call-start
  953.5 113.7 %all-reduce.26.cloned.1.call-done = bf16[256,256]{0,1:T(8,128)(2,1)} async-done(((bf16[256,256]{0,1:T(8,128)(2,1)}), bf16[256,256]{0,1:T(8,128)(2,1)}) %all-reduce.26.cloned.1.call-update) | async-done | bytes 131088 | tf_op jit(solution)/shard_map/psum | solution.py:9
  1067.2 0.3 fusion
  1067.5 0.7 slice_bitcast_fusion.5
  1068.3 0.0 all-reduce.30.cloned.1.call-start
  1068.3 209.2 %all-reduce.28.cloned.1.call-done = f32[256,256]{1,0:T(8,128)} async-done(((f32[256,256]{1,0:T(8,128)}), f32[256,256]{1,0:T(8,128)}) %all-reduce.28.cloned.1.call-update) | async-done | bytes 262160 | tf_op jit(solution)/shard_map/psum | solution.py:59
  1277.5 2.0 fusion.14
  1279.5 0.0 all-reduce.32.cloned.1.call-start
  1279.6 0.1 copy.31
  1279.7 112.7 %all-reduce.30.cloned.1.call-done = bf16[256,256]{0,1:T(8,128)(2,1)} async-done(((bf16[256,256]{0,1:T(8,128)(2,1)}), bf16[256,256]{0,1:T(8,128)(2,1)}) %all-reduce.30.cloned.1.call-update) | async-done | bytes 131088 | tf_op jit(solution)/shard_map/psum | solution.py:9
  1392.4 1.2 fusion.2
  1393.6 0.7 slice_bitcast_fusion.2
  1394.3 0.0 all-reduce.34.cloned.1.call-start
  1394.4 208.1 %all-reduce.32.cloned.1.call-done = f32[256,256]{1,0:T(8,128)} async-done(((f32[256,256]{1,0:T(8,128)}), f32[256,256]{1,0:T(8,128)}) %all-reduce.32.cloned.1.call-update) | async-done | bytes 262160 | tf_op jit(solution)/shard_map/psum | solution.py:59
  1602.5 2.0 fusion.16
  1604.6 0.0 all-reduce.36.cloned.1.call-start
  1604.6 112.8 %all-reduce.34.cloned.1.call-done = bf16[256,256]{0,1:T(8,128)(2,1)} async-done(((bf16[256,256]{0,1:T(8,128)(2,1)}), bf16[256,256]{0,1:T(8,128)(2,1)}) %all-reduce.34.cloned.1.call-update) | async-done | bytes 131088 | tf_op jit(solution)/shard_map/psum | solution.py:9
  1717.4 1.6 fusion.10
  1719.0 0.0 all-reduce.38.cloned.1.call-start
  1719.1 0.7 maximum_bitcast_fusion
  1719.8 207.8 %all-reduce.36.cloned.1.call-done = f32[256,256]{1,0:T(8,128)} async-done(((f32[256,256]{1,0:T(8,128)}), f32[256,256]{1,0:T(8,128)}) %all-reduce.36.cloned.1.call-update) | async-done | bytes 262160 | tf_op jit(solution)/shard_map/psum | solution.py:59
  1927.6 2.0 fusion.18
  1929.6 0.9 copy-done.3
  1930.5 112.0 %all-reduce.38.cloned.1.call-done = bf16[256,256]{0,1:T(8,128)(2,1)} async-done(((bf16[256,256]{0,1:T(8,128)(2,1)}), bf16[256,256]{0,1:T(8,128)(2,1)}) %all-reduce.38.cloned.1.call-update) | async-done | bytes 131088 | tf_op jit(solution)/shard_map/psum | solution.py:9
  2042.5 0.9 select_bitcast_fusion.1
  2043.5 0.8 copy.43
  (27 shorter events, 0.3 us)
Async XLA Ops:
  7.2 2.4 copy-start.2
  7.2 204.9 %all-reduce.14.cloned.1.call-start = ((), (), s32[]{:S(2)}) async-start(), calls=%async_computation | async-start | bytes 262144 | tf_op jit(solution)/shard_map/psum | solution.py:9
  9.5 316.1 %all-reduce.16.cloned.1.call-start = ((), (), s32[]{:S(2)}) async-start(), calls=%async_computation.1 | async-start | bytes 524288 | tf_op jit(solution)/shard_map/psum | solution.py:38
  9.6 0.7 copy-start.6
  213.2 1.1 copy-start.1
  214.0 311.1 %all-reduce.18.cloned.1.call-start = ((), (), s32[]{:S(2)}) async-start(), calls=%async_computation.2 | async-start | bytes 262144 | tf_op jit(solution)/shard_map/psum | solution.py:9
  214.4 111.2 %copy-start = (bf16[2,1,256,256]{3,2,1,0:T(8,128)(2,1)S(1)}, bf16[2,1,256,256]{3,2,1,0:T(8,128)(2,1)}, u32[]{:S(2)}) copy-start(bf16[2,1,256,256]{3,2,1,0:T(8,128)(2,1)} %param.22) | copy-start | bytes 786436
  327.6 310.9 %all-reduce.20.cloned.1.call-start = ((), (), s32[]{:S(2)}) async-start(), calls=%async_computation.3 | async-start | bytes 524288 | tf_op jit(solution)/shard_map/psum | solution.py:38
  527.0 310.8 %all-reduce.22.cloned.1.call-start = ((), (), s32[]{:S(2)}) async-start(), calls=%async_computation.4 | async-start | bytes 262144 | tf_op jit(solution)/shard_map/psum | solution.py:9
  640.5 310.8 %all-reduce.24.cloned.1.call-start = ((), (), s32[]{:S(2)}) async-start(), calls=%async_computation.5 | async-start | bytes 524288 | tf_op jit(solution)/shard_map/psum | solution.py:38
  840.3 226.9 %all-reduce.26.cloned.1.call-start = ((), (), s32[]{:S(2)}) async-start(), calls=%async_computation.6 | async-start | bytes 262144 | tf_op jit(solution)/shard_map/psum | solution.py:9
  953.4 324.1 %all-reduce.28.cloned.1.call-start = ((), (), s32[]{:S(2)}) async-start(), calls=%async_computation.7 | async-start | bytes 524288 | tf_op jit(solution)/shard_map/psum | solution.py:59
  1068.3 324.1 %all-reduce.30.cloned.1.call-start = ((), (), s32[]{:S(2)}) async-start(), calls=%async_computation.8 | async-start | bytes 262144 | tf_op jit(solution)/shard_map/psum | solution.py:9
  1279.5 323.0 %all-reduce.32.cloned.1.call-start = ((), (), s32[]{:S(2)}) async-start(), calls=%async_computation.9 | async-start | bytes 524288 | tf_op jit(solution)/shard_map/psum | solution.py:59
  1394.3 323.1 %all-reduce.34.cloned.1.call-start = ((), (), s32[]{:S(2)}) async-start(), calls=%async_computation.10 | async-start | bytes 262144 | tf_op jit(solution)/shard_map/psum | solution.py:9
  1604.6 323.0 %all-reduce.36.cloned.1.call-start = ((), (), s32[]{:S(2)}) async-start(), calls=%async_computation.11 | async-start | bytes 524288 | tf_op jit(solution)/shard_map/psum | solution.py:59
  1719.0 323.5 %all-reduce.38.cloned.1.call-start = ((), (), s32[]{:S(2)}) async-start(), calls=%async_computation.12 | async-start | bytes 262144 | tf_op jit(solution)/shard_map/psum | solution.py:9
  1927.6 2.1 copy-start.4
  1929.6 0.9 copy-start.3
  1930.5 112.0 %copy-start.5 = (bf16[256,256]{0,1:T(8,128)(2,1)S(1)}, bf16[256,256]{0,1:T(8,128)(2,1)}, u32[]{:S(2)}) copy-start(bf16[256,256]{0,1:T(8,128)(2,1)} %all-reduce.34.cloned.1.call-done) | copy-start | bytes 393220
Sparse Core Ops, SparseCore 0:
  10.9 201.1 all-reduce.13
  216.1 109.4 all-reduce.15
  328.5 196.5 all-reduce.17
  529.0 109.4 all-reduce.19
  641.2 196.5 all-reduce.21
  841.8 109.4 all-reduce.23
  955.0 112.1 all-reduce.25
  1070.2 207.2 all-reduce.27
  1281.3 111.0 all-reduce.29
  1395.2 207.2 all-reduce.31
  1606.3 111.0 all-reduce.33
  1720.3 207.2 all-reduce.35
  1931.3 111.1 all-reduce.37
where the time goes:
time: 2050 us
  waiting for transfers between devices  2010 us (98%)
  matrix products  20.6 us (1%)
    psum x7, waiting for transfers between devices, broadcast(): return lax.psum(jnp.where(mine, value, jnp.zeros_like(value)), axis)  1050 us
    psum x3, waiting for transfers between devices, per_device(): total = lax.psum(backlog[m], 'row')  625 us
    psum x3, waiting for transfers between devices, per_device(): total = lax.psum(pending[slot], 'col')  333 us
  transfers between devices with their start and end apart: 13, of which 13 were waited for; matrix products, arithmetic and copies ran while one was open for 0% of the time, Pallas kernels for 0%

commit v1 on v0

v1 whole, which is shorter than its diff:
```python
import jax
import jax.numpy as jnp
from jax import lax
from jax.experimental import pallas as pl
from jax.experimental.pallas import tpu as pltpu
from jax.sharding import PartitionSpec as P

MESH = pl.DeviceIdType.MESH
NT = (((1,), (1,)), ((), ()))
NN = (((1,), (0,)), ((), ()))
Y_IN, P_IN, Y_ALL, X_IN, X_OTH, Q_IN, L_IN = 0, 3, 5, 7, 9, 11, 14


def exact_dot(lhs, inverse, dims):
    rows = lhs.shape[0]
    high = lhs.astype(jnp.bfloat16)
    rest = lhs - high.astype(jnp.float32)
    mid = rest.astype(jnp.bfloat16)
    low = (rest - mid.astype(jnp.float32)).astype(jnp.bfloat16)
    stacked = jnp.concatenate([high, mid, low], axis=0)
    out = lax.dot_general(stacked, inverse, dims, preferred_element_type=jnp.float32)
    return out[:rows] + (out[rows : 2 * rows] + out[2 * rows :])


def kernel(
    pattern, factor, dinv, rhs, out_y, out_x,
    blocks, b_t, y_own, x_own, y_in, p_out, p_in, acc, y_all, x_in, x_oth, q_acc, q_out, q_in,
    send_sem, recv_sem,
):
    r, c = lax.axis_index("row"), lax.axis_index("col")
    z, k = r // 2, r % 2
    h = z // 8
    s = r % 16
    kq, ql = c // 8, c % 8
    barrier = pltpu.get_barrier_semaphore()

    def signal(row, col):
        here = (row == r) & (col == c)

        @pl.when(jnp.logical_not(here))
        def _():
            pl.semaphore_signal(barrier, inc=1, device_id=(row, col), device_id_type=MESH)

    @pl.loop(0, 16)
    def _(p):
        signal(2 * ((z + p) % 16) + kq, s)
        signal(c + 16 * (p // 8), 8 * k + p % 8)

    @pl.loop(0, 16)
    def _(p):
        signal(r, (c + p) % 16)
        signal(2 * z + 1 - k, (c + p) % 16)

    def remote(src, dst, event, cls, row, col):
        return pltpu.make_async_remote_copy(
            src_ref=src, dst_ref=dst, send_sem=send_sem.at[event], recv_sem=recv_sem.at[cls],
            device_id=(row, col), device_id_type=MESH,
        )

    def send(src, dst, event, cls, row, col, here):
        @pl.when(here)
        def _():
            pltpu.make_async_copy(src, dst, recv_sem.at[cls]).start()

        @pl.when(jnp.logical_not(here))
        def _():
            remote(src, dst, event, cls, row, col).start()

    def arrived(buf, cls):
        remote(buf, buf, 0, cls, r, c).wait_recv()

    def sent(event, count, one_less):
        @pl.when(one_less)
        def _():
            if count > 1:
                d = y_all.at[0, pl.ds(0, count - 1)]
                remote(d, d, event, 0, r, c).wait_send()

        @pl.when(jnp.logical_not(one_less))
        def _():
            d = y_all.at[0, pl.ds(0, count)]
            remote(d, d, event, 0, r, c).wait_send()

    def to_column(src, level, half, event):
        def go(p, here):
            row = 2 * (8 * half + (z + p) % 8) + kq
            args = (src, y_in.at[level, ql], event, Y_IN + level, row, s)
            if here is None:
                remote(*args).start()
            else:
                send(*args, here)

        go(0, (half == h) & (kq == k) & (s == c))

        @pl.loop(1, 8)
        def _(p):
            go(p, None)

    def column_self(half):
        return (half == h) & (kq == k) & (s == c)

    def to_owner(slot, event):
        for kk in range(2):
            for p in range(1):
                send(p_out.at[slot, kk, ql], p_in.at[slot, c], event, P_IN + slot,
                     2 * z + kk, 8 * k + ql, (kk == k) & (kq == k))

        @pl.loop(1, 8)
        def _(p):
            part = (ql + p) % 8
            for kk in range(2):
                remote(p_out.at[slot, kk, part], p_in.at[slot, c], event, P_IN + slot,
                       2 * z + kk, 8 * k + part).start()

    def to_plane(src, dst, event, cls, core):
        send(src, dst, event, cls, 2 * z + core, c, core == k)

        @pl.loop(1, 16)
        def _(p):
            remote(src, dst, event, cls, 2 * z + core, (c + p) % 16).start()

    def to_supernode(slot, cls, half, event):
        row = 16 * half + c

        def go(part, here):
            args = (q_out.at[slot, part], q_in.at[cls, z % 8], event, Q_IN + cls, row, 8 * k + part)
            if here is None:
                remote(*args).start()
            else:
                send(*args, here)

        go(ql, supernode_self(half))

        @pl.loop(1, 8)
        def _(p):
            go((ql + p) % 8, None)

    def supernode_self(half):
        return (16 * half + c == r) & (kq == k)

    def product(level, kk, index):
        y = y_in[level].reshape(128, 256)
        return lax.dot_general(y, blocks[kk, index], NT, preferred_element_type=jnp.float32)

    def back_product(slot, index):
        total = None
        for kk in range(2):
            x = x_in[slot, kk].reshape(128, 256)
            term = lax.dot_general(x, blocks[kk, index], NN, preferred_element_type=jnp.float32)
            total = term if total is None else total + term
        return total

    def total_of(buf):
        return jnp.sum(buf[...].astype(jnp.float32), axis=0)

    def solve_forward(slot):
        arrived(p_in.at[slot], P_IN + slot)
        residue = b_t[slot] - total_of(p_in.at[slot])
        y_own[slot] = exact_dot(residue, dinv[slot], NT).astype(jnp.bfloat16)

    def put_q(slot, value):
        q_out[slot] = value.astype(jnp.bfloat16).reshape(8, 16, 256)

    def natural(value):
        return value.astype(jnp.float32).T.astype(jnp.bfloat16)

    def write_y(slot):
        arrived(y_all.at[slot], Y_ALL + slot)
        out_y[slot] = natural(y_all[slot].reshape(256, 256))

    def write_x(slot):
        arrived(x_oth.at[slot], X_OTH + slot)
        mine = x_in[slot, k].reshape(128, 256)
        other = x_oth[slot].reshape(128, 256)

        @pl.when(k == 0)
        def _():
            out_x[slot] = natural(jnp.concatenate([mine, other], axis=0))

        @pl.when(k == 1)
        def _():
            out_x[slot] = natural(jnp.concatenate([other, mine], axis=0))

    def spread_x(slot, event):
        to_plane(x_own.at[slot], x_in.at[slot, k, ql], event, X_IN + slot, kq)

        @pl.when(kq != k)
        def _():
            to_plane(x_own.at[slot], x_oth.at[slot, ql], event + 1, X_OTH + slot, k)

    def spread_x_sent(event):
        sent(event, 16, kq == k)

        @pl.when(kq != k)
        def _():
            sent(event + 1, 15, False)

    for slot in range(2):
        q_acc[...] = rhs[slot].T
        b_t[slot] = q_acc[pl.ds(pl.multiple_of(16 * c, 16), 16), :]

    @pl.when(h == 0)
    def _():
        y_own[0] = exact_dot(b_t[0], dinv[0], NT).astype(jnp.bfloat16)

    places = ((0, 0), (1, 0), (1, 1), (1, 2))
    for index, (slot, level) in enumerate(places):
        weight = pattern[slot, level].astype(jnp.float32)
        blocks[k, index] = (factor[slot, level].astype(jnp.float32) * weight).astype(jnp.bfloat16)

    pl.semaphore_wait(barrier, 63 - 2 * ((kq == k) & (s == c)).astype(jnp.int32))

    swap = remote(blocks.at[k], blocks.at[k], 0, L_IN, 2 * z + 1 - k, c)

    @pl.when(h == 0)
    def _():
        to_column(y_own.at[0], 0, 1, 1)
        swap.start()
        to_column(y_own.at[0], 0, 0, 2)
        out_y[0] = exact_dot(rhs[0].T, dinv[0], NT).T.astype(jnp.bfloat16)
        arrived(blocks.at[1 - k], L_IN)
        arrived(y_in.at[0], Y_IN)
        for kk in range(2):
            acc[kk] = product(0, kk, 1)
        arrived(y_in.at[1], Y_IN + 1)
        for kk in range(2):
            value = acc[kk] + product(1, kk, 2)
            p_out[1, kk] = value.astype(jnp.bfloat16).reshape(8, 16, 256)
        to_owner(1, 3)
        solve_forward(1)
        to_column(y_own.at[1], 2, 1, 4)
        to_plane(y_own.at[1], y_all.at[1, c], 5, Y_ALL + 1, k)
        write_y(1)
        arrived(q_in.at[2], Q_IN + 2)
        residue = y_own[1].astype(jnp.float32) - total_of(q_in.at[2])
        x_own[1] = exact_dot(residue, dinv[1], NN).astype(jnp.bfloat16)
        spread_x(1, 6)
        arrived(x_in.at[1], X_IN + 1)
        put_q(0, back_product(1, 2))
        to_supernode(0, 1, 1, 8)
        put_q(1, back_product(1, 1))
        to_supernode(1, 0, 0, 9)
        write_x(1)
        arrived(q_in.at[0], Q_IN)
        residue = y_own[0].astype(jnp.float32) - total_of(q_in.at[0])
        arrived(q_in.at[1], Q_IN + 1)
        residue = residue - total_of(q_in.at[1])
        x_own[0] = exact_dot(residue, dinv[0], NN).astype(jnp.bfloat16)

        @pl.when(kq == k)
        def _():
            to_plane(x_own.at[0], x_in.at[0, k, ql], 10, X_IN, k)

        @pl.when(kq != k)
        def _():
            to_plane(x_own.at[0], x_oth.at[0, ql], 10, X_OTH, k)

        arrived(x_in.at[0, k], X_IN)
        write_x(0)
        swap.wait_send()
        sent(1, 8, False)
        sent(2, 8, column_self(0))
        sent(3, 16, kq == k)
        sent(4, 8, False)
        sent(5, 15, False)
        spread_x_sent(6)
        sent(8, 8, False)
        sent(9, 8, supernode_self(0))
        sent(10, 15, False)

    @pl.when(h == 1)
    def _():
        swap.start()
        arrived(blocks.at[1 - k], L_IN)
        arrived(y_in.at[0], Y_IN)
        for kk in range(2):
            p_out[0, kk] = product(0, kk, 0).astype(jnp.bfloat16).reshape(8, 16, 256)
        to_owner(0, 1)
        solve_forward(0)
        to_column(y_own.at[0], 1, 0, 2)
        to_column(y_own.at[0], 1, 1, 3)
        to_plane(y_own.at[0], y_all.at[0, c], 4, Y_ALL, k)
        for kk in range(2):
            acc[kk] = product(0, kk, 1)
        arrived(y_in.at[1], Y_IN + 1)
        for kk in range(2):
            acc[kk] += product(1, kk, 2)
        write_y(0)
        arrived(y_in.at[2], Y_IN + 2)
        for kk in range(2):
            value = acc[kk] + product(2, kk, 3)
            p_out[1, kk] = value.astype(jnp.bfloat16).reshape(8, 16, 256)
        to_owner(1, 5)
        solve_forward(1)
        x_own[1] = exact_dot(y_own[1].astype(jnp.float32), dinv[1], NN).astype(jnp.bfloat16)
        spread_x(1, 6)
        to_plane(y_own.at[1], y_all.at[1, c], 8, Y_ALL + 1, k)
        arrived(x_in.at[1], X_IN + 1)
        put_q(0, back_product(1, 3))
        to_supernode(0, 2, 0, 9)
        put_q(1, back_product(1, 2))
        to_supernode(1, 0, 1, 10)
        acc[0] = back_product(1, 1)
        write_y(1)
        write_x(1)
        arrived(q_in.at[0], Q_IN)
        residue = y_own[0].astype(jnp.float32) - total_of(q_in.at[0])
        arrived(q_in.at[1], Q_IN + 1)
        residue = residue - total_of(q_in.at[1])
        x_own[0] = exact_dot(residue, dinv[0], NN).astype(jnp.bfloat16)
        spread_x(0, 11)
        arrived(x_in.at[0], X_IN)
        put_q(2, acc[0] + back_product(0, 0))
        to_supernode(2, 1, 0, 13)
        write_x(0)
        swap.wait_send()
        sent(1, 16, kq == k)
        sent(2, 8, False)
        sent(3, 8, column_self(1))
        sent(4, 15, False)
        sent(5, 16, kq == k)
        spread_x_sent(6)
        sent(8, 15, False)
        sent(9, 8, False)
        sent(10, 8, supernode_self(1))
        spread_x_sent(11)
        sent(13, 8, False)


def per_device(factor, pattern, dinv, rhs):
    bf16, f32 = jnp.bfloat16, jnp.float32
    vmem = pl.BlockSpec(memory_space=pltpu.VMEM)
    out = jax.ShapeDtypeStruct((2, 256, 256), bf16)
    forward, back = pl.pallas_call(
        kernel,
        out_shape=(out, out),
        in_specs=[pl.BlockSpec(memory_space=pltpu.SMEM), vmem, vmem, vmem],
        out_specs=(vmem, vmem),
        scratch_shapes=[
            pltpu.VMEM((2, 4, 256, 256), bf16),
            pltpu.VMEM((2, 16, 256), f32),
            pltpu.VMEM((2, 16, 256), bf16),
            pltpu.VMEM((2, 16, 256), bf16),
            pltpu.VMEM((3, 8, 16, 256), bf16),
            pltpu.VMEM((2, 2, 8, 16, 256), bf16),
            pltpu.VMEM((2, 16, 16, 256), bf16),
            pltpu.VMEM((2, 128, 256), f32),
            pltpu.VMEM((2, 16, 16, 256), bf16),
            pltpu.VMEM((2, 2, 8, 16, 256), bf16),
            pltpu.VMEM((2, 8, 16, 256), bf16),
            pltpu.VMEM((256, 256), f32),
            pltpu.VMEM((3, 8, 16, 256), bf16),
            pltpu.VMEM((3, 8, 16, 256), bf16),
            pltpu.SemaphoreType.DMA((14,)),
            pltpu.SemaphoreType.DMA((15,)),
        ],
        compiler_params=pltpu.CompilerParams(
            collective_id=0, has_side_effects=True, vmem_limit_bytes=32 * 1024 * 1024
        ),
        cost_estimate=pl.CostEstimate(flops=600_000_000, bytes_accessed=3_000_000, transcendentals=0),
    )(pattern[:, 0, :, 0], factor[:, 0, :, 0], dinv[:, 0], rhs[:, 0])
    return forward[:, None], back[:, None]


def solution(mesh):
    placed = (
        P(None, "row", None, "col", None, None),
        P(None, "row", None, "col"),
        P(None, "row", None, None),
        P(None, "row", None, None),
    )
    return jax.shard_map(
        per_device,
        mesh=mesh,
        in_specs=placed,
        out_specs=(P(None, "row", None, None), P(None, "row", None, None)),
        check_vma=False,
    )
```

time: 2050 us -> 130 us (0.06)
  waiting for transfers between devices: 2010 us -> 0 us
  Pallas kernels: 0 us -> 124 us
  matrix products: 20.6 us -> 0 us
    psum x13 -> x0, waiting for transfers between devices: 2010 us -> none  [the longest x7 1050 us: broadcast(): return lax.psum(jnp.where(mine, value, jnp.zeros_like(value)), axis)]
    pallas_call x0 -> x1, Pallas kernels: none -> 124 us  [per_device(): pl.pallas_call(kernel, out_shape=(out, out), in_specs=[pl.BlockSpec(memor...]
    dot_general x14 -> x0, matrix products: 20.6 us -> none  [the longest x4 6.91 us: per_device(): jnp.dot(inverse_blocks[slot].T, residue, precision=upper_limit)]
  transfers between devices with their start and end apart: 13 -> 0, of which waited for: 13 -> 0; matrix products, arithmetic and copies ran while one was open for 0% -> 0% of each run, Pallas kernels for 0% -> 0%
where the time goes in v1:
time: 130 us
  Pallas kernels  124 us (95%)
  local copies, waits for them, and re-layouts  5.29 us (4%)
    pallas_call x1, Pallas kernels, per_device(): pl.pallas_call(kernel, out_shape=(out, out), in_specs=[pl.BlockSpec(memor...  124 us
    unnamed x10, local copies, waits for them, and re-layouts  5.29 us

profile of v1, /device:TPU:1, one launch (start us, length us, event | category | flops | bytes accessed | tf_op | source)
XLA Modules:
  0.0 129.6 jit_solution(16984811152403732625)
XLA Ops:
  0.6 0.0 copy-start.3
  0.6 0.7 copy-done.3
  1.3 0.0 copy-start
  1.3 1.2 copy-done
  2.5 0.0 copy-start.1
  2.5 1.0 copy-done.1
  3.6 0.0 copy-start.2
  3.6 0.9 copy-done.2
  4.5 123.6 %shard_map.59 = (bf16[2,256,256]{2,1,0:T(8,128)(2,1)S(1)}, bf16[2,256,256]{2,1,0:T(8,128)(2,1)S(1)}) custom-call(s32[2,4]{1,0:T(2,128)S(1)} %bitcast.15, bf16[2,4,256,256]{3,2,1,0:T(8,128)(2,1)S(1)} %bitcast.12, bf16[2,256,256]{2,1,0:T(8,128)(2,1)S(1)} %bitcast.14, f32[2,256,256]{2,1,0:T(8,128)S(1)} %bitcast.13), custom_call_target="tpu_custom_call" | custom-call | flops 600000000 | bytes 3000000 | tf_op jit(solution)/shard_map/pallas_call | solution.py:334
  128.2 0.7 copy.10
  128.9 0.7 copy.11
Async XLA Ops:
  0.6 0.7 copy-start.3
  1.3 1.2 copy-start
  2.5 1.0 copy-start.1
  3.6 0.9 copy-start.2

commit v2 on v1

v2 whole, which is shorter than its diff:
```python
import jax
import jax.numpy as jnp
from jax import lax
from jax.experimental import pallas as pl
from jax.experimental.pallas import tpu as pltpu
from jax.sharding import PartitionSpec as P

MESH = pl.DeviceIdType.MESH
NT = (((1,), (1,)), ((), ()))
NN = (((1,), (0,)), ((), ()))
PLACES = ((0, 0), (1, 0), (1, 1), (1, 2))
Y_IN, P_IN, Y_ALL, X_IN, X_ALL, Q_IN, L_IN, G_IN = 0, 3, 5, 7, 9, 11, 14, 18


def exact_dot(lhs, inverse, dims):
    rows = lhs.shape[0]
    high = lhs.astype(jnp.bfloat16)
    rest = lhs - high.astype(jnp.float32)
    mid = rest.astype(jnp.bfloat16)
    low = (rest - mid.astype(jnp.float32)).astype(jnp.bfloat16)
    stacked = jnp.concatenate([high, mid, low], axis=0)
    out = lax.dot_general(stacked, inverse, dims, preferred_element_type=jnp.float32)
    return out[:rows] + (out[rows : 2 * rows] + out[2 * rows :])


def kernel(
    pattern_hbm, factor_hbm, dinv_hbm, rhs_hbm, out_y, out_x,
    pattern, factor, dinv, rhs, blocks, b_t, y_own, x_own, y_in, p_out, p_in, acc,
    y_all, x_in, x_all, turned, q_acc, q_out, q_in,
    send_sem, recv_sem, load_sem,
):
    r, c = lax.axis_index("row"), lax.axis_index("col")
    z, k = r // 2, r % 2
    h = z // 8
    s = r % 16
    x, y = c // 4, c % 4
    kq, ql = y // 2, y % 2
    barrier = pltpu.get_barrier_semaphore()
    loads = [
        pltpu.make_async_copy(source, target, load_sem.at[i])
        for i, (source, target) in enumerate(
            ((rhs_hbm, rhs), (dinv_hbm, dinv), (pattern_hbm, pattern))
            + tuple((factor_hbm.at[slot, level], factor.at[j]) for j, (slot, level) in enumerate(PLACES))
        )
    ]
    for load in loads:
        load.start()

    def signal(row, col):
        here = (row == r) & (col == c)

        @pl.when(jnp.logical_not(here))
        def _():
            pl.semaphore_signal(barrier, inc=1, device_id=(row, col), device_id_type=MESH)

    @pl.loop(0, 16)
    def _(p):
        signal(2 * ((z + p) % 16) + kq, 4 * x + s % 4)
        signal(16 * (p // 8) + 4 * (p // 2 % 4) + y, 4 * x + 2 * k + p % 2)

    @pl.loop(0, 16)
    def _(p):
        signal(r, (c + p) % 16)
        signal(2 * z + 1 - k, (c + p) % 16)

    def remote(src, dst, event, cls, row, col):
        return pltpu.make_async_remote_copy(
            src_ref=src, dst_ref=dst, send_sem=send_sem.at[event], recv_sem=recv_sem.at[cls],
            device_id=(row, col), device_id_type=MESH,
        )

    def send(src, dst, event, cls, row, col, here):
        @pl.when(here)
        def _():
            pltpu.make_async_copy(src, dst, recv_sem.at[cls]).start()

        @pl.when(jnp.logical_not(here))
        def _():
            remote(src, dst, event, cls, row, col).start()

    def arrived(buf, cls):
        remote(buf, buf, 0, cls, r, c).wait_recv()

    def sent(event, count, one_less):
        @pl.when(one_less)
        def _():
            if count > 1:
                d = y_all.at[0, pl.ds(0, count - 1)]
                remote(d, d, event, 0, r, c).wait_send()

        @pl.when(jnp.logical_not(one_less))
        def _():
            d = y_all.at[0, pl.ds(0, count)]
            remote(d, d, event, 0, r, c).wait_send()

    def to_column(src, level, half, event):
        def go(p, here):
            row = 2 * (8 * half + (z + p) % 8) + kq
            args = (src, y_in.at[level, s // 4, ql], event, Y_IN + level, row, 4 * x + s % 4)
            if here is None:
                remote(*args).start()
            else:
                send(*args, here)

        go(0, own_column(half))

        @pl.loop(1, 8)
        def _(p):
            go(p, None)

    def own_column(half):
        return (half == h) & (kq == k) & (s % 4 == y)

    def to_owner(slot, event):
        for p in range(2):
            part = (ql + p) % 2
            for kk in range(2):
                args = (p_out.at[slot, kk, part], p_in.at[slot, y], event, P_IN + slot,
                        2 * z + kk, 4 * x + 2 * k + part)
                if p == 0:
                    send(*args, (kk == k) & (kq == k))
                else:
                    remote(*args).start()

    def to_line(src, slot, event):
        for p in range(4):
            args = (src, x_in.at[slot, k, ql], event, X_IN + slot, 2 * z + kq, 4 * x + (y + p) % 4)
            if p == 0:
                send(*args, kq == k)
            else:
                remote(*args).start()

    def to_plane(src, dst, event, cls):
        pltpu.make_async_copy(src, dst, recv_sem.at[cls]).start()

        @pl.loop(1, 16)
        def _(p):
            remote(src, dst, event, cls, r, (c + p) % 16).start()

    def to_supernode(slot, cls, half, event):
        def go(p, here):
            line, part = (s // 4 + p // 2) % 4, (ql + p) % 2
            args = (q_out.at[slot, line, part], q_in.at[cls, z % 8], event, Q_IN + cls,
                    16 * half + 4 * line + y, 4 * x + 2 * k + part)
            if here is None:
                remote(*args).start()
            else:
                send(*args, here)

        go(0, own_column(half))

        @pl.loop(1, 8)
        def _(p):
            go(p, None)

    def gather(index):
        for p in range(1, 4):
            block = blocks.at[k, index, x]
            remote(block, block, 14 + index, G_IN + index, r, 4 * ((x + p) % 4) + y).start()

    def swap(index):
        return remote(blocks.at[k, index], blocks.at[k, index], 18 + index, L_IN + index, 2 * z + 1 - k, c)

    def gathered(index):
        arrived(blocks.at[k, index, pl.ds(0, 3)], G_IN + index)
        swap(index).start()

    def factor_ready(index):
        arrived(blocks.at[1 - k, index], L_IN + index)

    def factor_sent(index):
        d = blocks.at[k, index, pl.ds(0, 3)]
        remote(d, d, 14 + index, 0, r, c).wait_send()
        swap(index).wait_send()

    def product(level, kk, index):
        total = None
        for line in range(4):
            term = lax.dot_general(
                y_in[level, line].reshape(32, 256), blocks[kk, index, line], NT,
                preferred_element_type=jnp.float32,
            )
            total = term if total is None else total + term
        return total

    def back_product(slot, index, line):
        total = None
        for kk in range(2):
            term = lax.dot_general(
                x_in[slot, kk].reshape(32, 256), blocks[kk, index, line], NN,
                preferred_element_type=jnp.float32,
            )
            total = term if total is None else total + term
        return total

    def total_of(buf):
        return jnp.sum(buf[...].astype(jnp.float32), axis=0)

    def solve_forward(slot):
        arrived(p_in.at[slot], P_IN + slot)
        residue = b_t[slot] - total_of(p_in.at[slot])
        y_own[slot] = exact_dot(residue, dinv[slot], NT).astype(jnp.bfloat16)

    def put_p(slot, kk, value):
        p_out[slot, kk] = value.astype(jnp.bfloat16).reshape(2, 16, 256)

    def put_q(slot, line, value):
        q_out[slot, line] = value.astype(jnp.bfloat16).reshape(2, 16, 256)

    def natural(value):
        return value.reshape(256, 256).astype(jnp.float32).T.astype(jnp.bfloat16)

    def write_y(slot):
        arrived(y_all.at[slot], Y_ALL + slot)
        out_y[slot] = natural(y_all[slot])

    def write_x(slot):
        arrived(x_all.at[slot], X_ALL + slot)
        out_x[slot] = natural(x_all[slot])

    loads[0].wait()
    for slot in range(2):
        turned[...] = rhs[slot].T
        b_t[slot] = turned[pl.ds(pl.multiple_of(16 * c, 16), 16), :]

    loads[1].wait()

    @pl.when(h == 0)
    def _():
        y_own[0] = exact_dot(b_t[0], dinv[0], NT).astype(jnp.bfloat16)

    for load in loads[2:]:
        load.wait()
    for index, (slot, level) in enumerate(PLACES):
        weight = pattern[slot, level].astype(jnp.float32)
        blocks[k, index, x] = (factor[index].astype(jnp.float32) * weight).astype(jnp.bfloat16)

    pl.semaphore_wait(barrier, 63 - 2 * ((kq == k) & (s % 4 == y)).astype(jnp.int32))

    @pl.when(h == 0)
    def _():
        to_column(y_own.at[0], 0, 1, 1)
        gather(1)
        gather(2)
        sent(1, 8, False)
        to_column(y_own.at[0], 0, 0, 2)
        out_y[0] = exact_dot(rhs[0].T, dinv[0], NT).T.astype(jnp.bfloat16)
        gathered(1)
        gathered(2)
        factor_ready(1)
        arrived(y_in.at[0], Y_IN)
        for kk in range(2):
            acc[kk] = product(0, kk, 1)
        factor_ready(2)
        arrived(y_in.at[1], Y_IN + 1)
        for kk in range(2):
            put_p(1, kk, acc[kk] + product(1, kk, 2))
        to_owner(1, 3)
        solve_forward(1)
        to_column(y_own.at[1], 2, 1, 4)
        sent(4, 8, False)
        to_plane(y_own.at[1], y_all.at[1, c], 5, Y_ALL + 1)
        write_y(1)
        arrived(q_in.at[2], Q_IN + 2)
        residue = y_own[1].astype(jnp.float32) - total_of(q_in.at[2])
        x_own[1] = exact_dot(residue, dinv[1], NN).astype(jnp.bfloat16)
        to_line(x_own.at[1], 1, 6)
        arrived(x_in.at[1], X_IN + 1)
        for line in range(4):
            put_q(0, line, back_product(1, 2, line))
        to_supernode(0, 1, 1, 8)
        for line in range(4):
            put_q(1, line, back_product(1, 1, line))
        to_supernode(1, 0, 0, 9)
        to_plane(x_own.at[1], x_all.at[1, c], 7, X_ALL + 1)
        write_x(1)
        arrived(q_in.at[0], Q_IN)
        residue = y_own[0].astype(jnp.float32) - total_of(q_in.at[0])
        arrived(q_in.at[1], Q_IN + 1)
        residue = residue - total_of(q_in.at[1])
        x_own[0] = exact_dot(residue, dinv[0], NN).astype(jnp.bfloat16)
        to_plane(x_own.at[0], x_all.at[0, c], 10, X_ALL)
        write_x(0)
        for index in (1, 2):
            factor_sent(index)
        sent(2, 8, own_column(0))
        sent(3, 4, kq == k)
        sent(5, 15, False)
        sent(6, 4, kq == k)
        sent(7, 15, False)
        sent(8, 8, False)
        sent(9, 8, own_column(0))
        sent(10, 15, False)

    @pl.when(h == 1)
    def _():
        gather(0)
        gathered(0)
        for index in range(1, 4):
            gather(index)
        factor_ready(0)
        arrived(y_in.at[0], Y_IN)
        for kk in range(2):
            put_p(0, kk, product(0, kk, 0))
        to_owner(0, 1)
        solve_forward(0)
        to_column(y_own.at[0], 1, 0, 2)
        sent(2, 8, False)
        to_column(y_own.at[0], 1, 1, 3)
        to_plane(y_own.at[0], y_all.at[0, c], 4, Y_ALL)
        for index in range(1, 4):
            gathered(index)
        factor_ready(1)
        for kk in range(2):
            acc[kk] = product(0, kk, 1)
        factor_ready(2)
        arrived(y_in.at[1], Y_IN + 1)
        for kk in range(2):
            acc[kk] += product(1, kk, 2)
        write_y(0)
        factor_ready(3)
        arrived(y_in.at[2], Y_IN + 2)
        for kk in range(2):
            put_p(1, kk, acc[kk] + product(2, kk, 3))
        to_owner(1, 5)
        solve_forward(1)
        x_own[1] = exact_dot(y_own[1].astype(jnp.float32), dinv[1], NN).astype(jnp.bfloat16)
        to_line(x_own.at[1], 1, 6)
        arrived(x_in.at[1], X_IN + 1)
        for line in range(4):
            put_q(0, line, back_product(1, 3, line))
        to_supernode(0, 2, 0, 9)
        for line in range(4):
            put_q(1, line, back_product(1, 2, line))
        to_supernode(1, 0, 1, 10)
        for line in range(4):
            q_acc[line] = back_product(1, 1, line)
        to_plane(y_own.at[1], y_all.at[1, c], 8, Y_ALL + 1)
        to_plane(x_own.at[1], x_all.at[1, c], 7, X_ALL + 1)
        write_y(1)
        write_x(1)
        arrived(q_in.at[0], Q_IN)
        residue = y_own[0].astype(jnp.float32) - total_of(q_in.at[0])
        arrived(q_in.at[1], Q_IN + 1)
        residue = residue - total_of(q_in.at[1])
        x_own[0] = exact_dot(residue, dinv[0], NN).astype(jnp.bfloat16)
        to_line(x_own.at[0], 0, 11)
        arrived(x_in.at[0], X_IN)
        for line in range(4):
            put_q(2, line, q_acc[line] + back_product(0, 0, line))
        to_supernode(2, 1, 0, 13)
        to_plane(x_own.at[0], x_all.at[0, c], 12, X_ALL)
        write_x(0)
        for index in range(4):
            factor_sent(index)
        sent(1, 4, kq == k)
        sent(3, 8, own_column(1))
        sent(4, 15, False)
        sent(5, 4, kq == k)
        sent(6, 4, kq == k)
        sent(7, 15, False)
        sent(8, 15, False)
        sent(9, 8, False)
        sent(10, 8, own_column(1))
        sent(11, 4, kq == k)
        sent(12, 15, False)
        sent(13, 8, False)


def per_device(factor, pattern, dinv, rhs):
    bf16, f32 = jnp.bfloat16, jnp.float32
    vmem = pl.BlockSpec(memory_space=pltpu.VMEM)
    out = jax.ShapeDtypeStruct((2, 256, 256), bf16)
    forward, back = pl.pallas_call(
        kernel,
        out_shape=(out, out),
        in_specs=[pl.BlockSpec(memory_space=pltpu.HBM)] * 4,
        out_specs=(vmem, vmem),
        scratch_shapes=[
            pltpu.SMEM((2, 4), jnp.int32),
            pltpu.VMEM((4, 256, 256), bf16),
            pltpu.VMEM((2, 256, 256), bf16),
            pltpu.VMEM((2, 256, 256), f32),
            pltpu.VMEM((2, 4, 4, 256, 256), bf16),
            pltpu.VMEM((2, 16, 256), f32),
            pltpu.VMEM((2, 16, 256), bf16),
            pltpu.VMEM((2, 16, 256), bf16),
            pltpu.VMEM((3, 4, 2, 16, 256), bf16),
            pltpu.VMEM((2, 2, 2, 16, 256), bf16),
            pltpu.VMEM((2, 4, 16, 256), bf16),
            pltpu.VMEM((2, 32, 256), f32),
            pltpu.VMEM((2, 16, 16, 256), bf16),
            pltpu.VMEM((2, 2, 2, 16, 256), bf16),
            pltpu.VMEM((2, 16, 16, 256), bf16),
            pltpu.VMEM((256, 256), f32),
            pltpu.VMEM((4, 32, 256), f32),
            pltpu.VMEM((3, 4, 2, 16, 256), bf16),
            pltpu.VMEM((3, 8, 16, 256), bf16),
            pltpu.SemaphoreType.DMA((22,)),
            pltpu.SemaphoreType.DMA((22,)),
            pltpu.SemaphoreType.DMA((7,)),
        ],
        compiler_params=pltpu.CompilerParams(
            collective_id=0, has_side_effects=True, vmem_limit_bytes=60 * 1024 * 1024
        ),
        cost_estimate=pl.CostEstimate(flops=600_000_000, bytes_accessed=3_000_000, transcendentals=0),
    )(pattern[:, 0, :, 0], factor[:, 0, :, 0], dinv[:, 0], rhs[:, 0])
    return forward[:, None], back[:, None]


def solution(mesh):
    placed = (
        P(None, "row", None, "col", None, None),
        P(None, "row", None, "col"),
        P(None, "row", None, None),
        P(None, "row", None, None),
    )
    return jax.shard_map(
        per_device,
        mesh=mesh,
        in_specs=placed,
        out_specs=(P(None, "row", None, None), P(None, "row", None, None)),
        check_vma=False,
    )
```

time: 130 us -> 108 us (0.83)
  Pallas kernels: 124 us -> 104 us
  local copies, waits for them, and re-layouts: 5.29 us -> 2.42 us
    pallas_call x1, Pallas kernels: 124 us -> 104 us  [per_device(): pl.pallas_call(kernel, out_shape=(out, out), in_specs=[pl.BlockSpec(memor...]
    unnamed x10 -> x4, local copies, waits for them, and re-layouts: 5.29 us -> 2.42 us
where the time goes in v2:
time: 108 us; the launch traced here: 107 us
  Pallas kernels  104 us (96%)
  local copies, waits for them, and re-layouts  2.42 us (2%)
    pallas_call x1, Pallas kernels, per_device(): pl.pallas_call(kernel, out_shape=(out, out), in_specs=[pl.BlockSpec(memor...  104 us
    unnamed x4, local copies, waits for them, and re-layouts  2.42 us

profile of v2, /device:TPU:1, one launch (start us, length us, event | category | flops | bytes accessed | tf_op | source)
XLA Modules:
  0.0 106.7 jit_solution(343519673426521052)
XLA Ops:
  0.6 103.7 %shard_map.59 = (bf16[2,256,256]{2,1,0:T(8,128)(2,1)}, bf16[2,256,256]{2,1,0:T(8,128)(2,1)}) custom-call(s32[2,4]{1,0:T(2,128)} %bitcast.15, bf16[2,4,256,256]{3,2,1,0:T(8,128)(2,1)} %bitcast.12, bf16[2,256,256]{2,1,0:T(8,128)(2,1)} %bitcast.14, f32[2,256,256]{2,1,0:T(8,128)} %bitcast.13), custom_call_target="tpu_custom_call" | custom-call | flops 600000000 | bytes 3000000 | tf_op jit(solution)/shard_map/pallas_call | solution.py:374
  104.3 0.0 copy-start
  104.3 1.7 %copy.10 = bf16[2,1,256,256]{3,2,1,0:T(8,128)(2,1)} copy(bf16[2,1,256,256]{3,2,1,0:T(8,128)(2,1)} %bitcast.11) | data formatting | bytes 524288
  106.0 0.0 copy-done
  106.0 0.7 copy.11
Async XLA Ops:
  104.3 1.7 %copy-start = (bf16[2,256,256]{2,1,0:T(8,128)(2,1)S(1)}, bf16[2,256,256]{2,1,0:T(8,128)(2,1)}, u32[]{:S(2)}) copy-start(bf16[2,256,256]{2,1,0:T(8,128)(2,1)} %get-tuple-element.5) | copy-start | bytes 786436

commit v3 on v2

v3 whole, which is shorter than its diff:
```python
import jax
import jax.numpy as jnp
from jax import lax
from jax.experimental import pallas as pl
from jax.experimental.pallas import tpu as pltpu
from jax.sharding import PartitionSpec as P

MESH = pl.DeviceIdType.MESH
NT = (((1,), (1,)), ((), ()))
NN = (((1,), (0,)), ((), ()))
PLACES = ((0, 0), (1, 0), (1, 1), (1, 2))
Y_IN, P_IN, Y_ALL, X_IN, X_ALL, Q_IN, L_IN, G_IN, D_IN, B_IN, Y0_IN = 0, 3, 5, 7, 9, 11, 14, 18, 22, 23, 24


def exact_dot(lhs, inverse, dims):
    rows = lhs.shape[0]
    high = lhs.astype(jnp.bfloat16)
    rest = lhs - high.astype(jnp.float32)
    mid = rest.astype(jnp.bfloat16)
    low = (rest - mid.astype(jnp.float32)).astype(jnp.bfloat16)
    stacked = jnp.concatenate([high, mid, low], axis=0)
    out = lax.dot_general(stacked, inverse, dims, preferred_element_type=jnp.float32)
    return out[:rows] + (out[rows : 2 * rows] + out[2 * rows :])


def kernel(
    pattern_hbm, factor_hbm, dinv_hbm, rhs_hbm, out,
    pattern, factor, dinv, rhs, blocks, d_own, b_t, b_own, y_0, y_own, x_own, y_in, p_out, p_in, acc,
    full, x_in, turned, q_acc, q_out, q_in,
    send_sem, recv_sem, load_sem,
):
    r, c = lax.axis_index("row"), lax.axis_index("col")
    z, k = r // 2, r % 2
    h = z // 8
    s = r % 16
    x, y = c // 4, c % 4
    own = y // 2 == z % 2
    core_own = y % 2
    line_own = z % 8 // 2
    source = own & (k == core_own)
    barrier = pltpu.get_barrier_semaphore()
    loads = [
        pltpu.make_async_copy(source, target, load_sem.at[i])
        for i, (source, target) in enumerate(
            ((rhs_hbm, rhs), (dinv_hbm, dinv), (pattern_hbm, pattern))
            + tuple((factor_hbm.at[slot, level], factor.at[j]) for j, (slot, level) in enumerate(PLACES))
        )
    ]
    for load in loads:
        load.start()

    def signal(row, col):
        pl.semaphore_signal(barrier, inc=1, device_id=(row, col), device_id_type=MESH)

    @pl.loop(1, 32)
    def _(p):
        signal((r + p) % 32, c)

    @pl.loop(1, 16)
    def _(p):
        signal(r, (c + p) % 16)
        signal(2 * z + 1 - k, (c + p) % 16)

    def remote(src, dst, event, cls, row, col):
        return pltpu.make_async_remote_copy(
            src_ref=src, dst_ref=dst, send_sem=send_sem.at[event], recv_sem=recv_sem.at[cls],
            device_id=(row, col), device_id_type=MESH,
        )

    def send(src, dst, event, cls, row, col, here):
        @pl.when(here)
        def _():
            pltpu.make_async_copy(src, dst, recv_sem.at[cls]).start()

        @pl.when(jnp.logical_not(here))
        def _():
            remote(src, dst, event, cls, row, col).start()

    def arrived(buf, cls):
        remote(buf, buf, 0, cls, r, c).wait_recv()

    def sent(event, count):
        d = full.at[pl.ds(0, count)]
        remote(d, d, event, 0, r, c).wait_send()

    def sent_unless(here, event, count):
        @pl.when(here)
        def _():
            sent(event, count - 1)

        @pl.when(jnp.logical_not(here))
        def _():
            sent(event, count)

    def to_column(slot, level, half, event):
        def go(p, here):
            args = (y_own.at[slot], y_in.at[level, line_own], event, Y_IN + level,
                    2 * (8 * half + (z + p) % 8) + k, c)
            if here is None:
                remote(*args).start()
            else:
                send(*args, here)

        go(0, half == h)

        @pl.loop(1, 8)
        def _(p):
            go(p, None)

    def first_to_column(half, event):
        def go(p, core, here):
            args = (y_0.at[core], y_in.at[0, line_own], event, Y_IN,
                    2 * (8 * half + (z + p) % 8) + core, c)
            if here is None:
                remote(*args).start()
            else:
                send(*args, here)

        for core in range(2):
            go(0, core, (half == h) & (core == k))

        @pl.loop(1, 8)
        def _(p):
            for core in range(2):
                go(p, core, None)

    def to_owner(slot, event):
        for kk in range(2):
            send(p_out.at[slot, kk], p_in.at[slot, y], event, P_IN + slot, r, 4 * x + 2 * (z % 2) + kk,
                 own & (kk == core_own))

    def to_line(slot, event):
        pltpu.make_async_copy(x_own.at[slot], x_in.at[slot, core_own], recv_sem.at[X_IN + slot]).start()
        for p in range(1, 4):
            remote(x_own.at[slot], x_in.at[slot, core_own], event, X_IN + slot, r, 4 * x + (y + p) % 4).start()

    def to_plane(src, slot, event, cls):
        dst = full.at[8 * slot + 2 * x + k]
        row = 2 * z + core_own
        send(src, dst, event, cls, row, c, source)

        @pl.loop(1, 16)
        def _(p):
            remote(src, dst, event, cls, row, (c + p) % 16).start()

    def to_supernode(slot, cls, half, event):
        for p in range(4):
            line = (line_own + p) % 4
            args = (q_out.at[slot, line], q_in.at[cls, z % 8], event, Q_IN + cls,
                    2 * (8 * half + 2 * line + y // 2) + k, c)
            if p == 0:
                send(*args, own & (half == h))
            else:
                remote(*args).start()

    def share(core, start):
        pairs = [(dinv, d_own, D_IN), (b_t.at[core], b_own, B_IN)]
        for i, (src, dst, cls) in enumerate(pairs):
            if start:
                send(src, dst, 22 + i, cls, 2 * z + core, c, core == k)
            else:
                pl.when(core != k)(remote(src, dst, 22 + i, cls, 2 * z + core, c).wait_send)

    def gather(index):
        for p in range(1, 4):
            block = blocks.at[k, index, x]
            remote(block, block, 14 + index, G_IN + index, r, 4 * ((x + p) % 4) + y).start()

    def swap(index):
        return remote(blocks.at[k, index], blocks.at[k, index], 18 + index, L_IN + index, 2 * z + 1 - k, c)

    def gathered(index):
        arrived(blocks.at[k, index, pl.ds(0, 3)], G_IN + index)
        swap(index).start()

    def factor_ready(index):
        arrived(blocks.at[1 - k, index], L_IN + index)

    def factor_sent(index):
        d = blocks.at[k, index, pl.ds(0, 3)]
        remote(d, d, 14 + index, 0, r, c).wait_send()
        swap(index).wait_send()

    def product(level, kk, index):
        total = None
        for line in range(4):
            term = lax.dot_general(
                y_in[level, line], blocks[kk, index, line], NT,
                preferred_element_type=jnp.float32,
            )
            total = term if total is None else total + term
        return total

    def back_product(slot, index, line):
        total = None
        for kk in range(2):
            term = lax.dot_general(
                x_in[slot, kk], blocks[kk, index, line], NN,
                preferred_element_type=jnp.float32,
            )
            total = term if total is None else total + term
        return total

    def solve_forward(slot):
        arrived(p_in.at[slot], P_IN + slot)
        total = jnp.sum(p_in[slot].astype(jnp.float32), axis=0)
        y_own[slot] = exact_dot(b_own[slot] - total, d_own[slot], NT).astype(jnp.bfloat16)

    def back_total(cls):
        arrived(q_in.at[cls], Q_IN + cls)
        return jnp.sum(q_in[cls].astype(jnp.float32), axis=0)

    def solve_back(slot, *classes):
        residue = y_own[slot].astype(jnp.float32)
        for cls in classes:
            residue = residue - back_total(cls)
        x_own[slot] = exact_dot(residue, d_own[slot], NN).astype(jnp.bfloat16)

    def own_ready():
        arrived(d_own, D_IN)
        arrived(b_own, B_IN)

    def put_p(slot, kk, value):
        p_out[slot, kk] = value.astype(jnp.bfloat16)

    def put_q(slot, line, value):
        q_out[slot, line] = value.astype(jnp.bfloat16)

    def natural(slot):
        value = full[pl.ds(8 * slot, 8)].reshape(256, 256)
        return value.astype(jnp.float32).T.astype(jnp.bfloat16)

    def write_y(slot):
        arrived(full.at[pl.ds(8 * slot, 8)], Y_ALL + slot)
        out[0, slot] = natural(slot)

    def write_x(slot):
        arrived(full.at[pl.ds(16 + 8 * slot, 8)], X_ALL + slot)
        out[1, slot] = natural(2 + slot)

    loads[0].wait()
    for slot in range(2):
        turned[...] = rhs[slot].T
        for core in range(2):
            b_t[core, slot] = turned[pl.ds(pl.multiple_of(64 * x + 32 * core, 32), 32), :]

    loads[1].wait()

    @pl.when(h == 0)
    def _():
        for core in range(2):
            y_0[core] = exact_dot(b_t[core, 0], dinv[0], NT).astype(jnp.bfloat16)

    for load in loads[2:]:
        load.wait()
    for index, (slot, level) in enumerate(PLACES):
        weight = pattern[slot, level].astype(jnp.float32)
        blocks[k, index, x] = (factor[index].astype(jnp.float32) * weight).astype(jnp.bfloat16)

    pl.semaphore_wait(barrier, 61)

    @pl.when(h == 0)
    def _():
        @pl.when(source)
        def _():
            first_to_column(1, 1)
            for core in range(2):
                share(core, True)
                send(y_0.at[core], y_own.at[0], 0, Y0_IN, 2 * z + core, c, core == k)

        gather(1)
        gather(2)
        out[0, 0] = exact_dot(rhs[0].T, dinv[0], NT).T.astype(jnp.bfloat16)
        gathered(1)

        @pl.when(source)
        def _():
            sent(1, 16)
            first_to_column(0, 2)

        gathered(2)
        factor_ready(1)
        arrived(y_in.at[0], Y_IN)
        for kk in range(2):
            acc[kk] = product(0, kk, 1)
        factor_ready(2)
        arrived(y_in.at[1], Y_IN + 1)
        for kk in range(2):
            put_p(1, kk, acc[kk] + product(1, kk, 2))
        to_owner(1, 3)

        @pl.when(own)
        def _():
            own_ready()
            arrived(y_own.at[0], Y0_IN)
            solve_forward(1)
            to_column(1, 2, 1, 4)
            sent(4, 8)
            to_plane(y_own.at[1], 1, 5, Y_ALL + 1)

        write_y(1)

        @pl.when(own)
        def _():
            solve_back(1, 2)
            to_line(1, 6)

        arrived(x_in.at[1], X_IN + 1)
        for line in range(4):
            put_q(0, line, back_product(1, 2, line))
        to_supernode(0, 1, 1, 8)
        for line in range(4):
            put_q(1, line, back_product(1, 1, line))

        @pl.when(own)
        def _():
            to_plane(x_own.at[1], 3, 7, X_ALL + 1)

        to_supernode(1, 0, 0, 9)
        write_x(1)

        @pl.when(own)
        def _():
            solve_back(0, 0, 1)
            to_plane(x_own.at[0], 2, 10, X_ALL)

        write_x(0)
        for index in (1, 2):
            factor_sent(index)
        sent_unless(own, 3, 2)
        sent(8, 4)
        sent_unless(own, 9, 4)

        @pl.when(source)
        def _():
            sent(2, 15)
            sent(0, 1)
            for core in range(2):
                share(core, False)

        @pl.when(own)
        def _():
            sent_unless(source, 5, 16)
            sent(6, 3)
            sent_unless(source, 7, 16)
            sent_unless(source, 10, 16)

    @pl.when(h == 1)
    def _():
        gather(0)

        @pl.when(source)
        def _():
            for core in range(2):
                share(core, True)

        gathered(0)
        for index in range(1, 4):
            gather(index)
        factor_ready(0)
        arrived(y_in.at[0], Y_IN)
        for kk in range(2):
            put_p(0, kk, product(0, kk, 0))
        to_owner(0, 1)

        @pl.when(own)
        def _():
            own_ready()
            solve_forward(0)
            to_column(0, 1, 0, 2)
            sent(2, 8)
            to_plane(y_own.at[0], 0, 4, Y_ALL)

        for index in range(1, 4):
            gathered(index)
        factor_ready(1)
        for kk in range(2):
            acc[kk] = product(0, kk, 1)
        write_y(0)

        @pl.when(own)
        def _():
            to_column(0, 1, 1, 3)

        factor_ready(2)
        arrived(y_in.at[1], Y_IN + 1)
        for kk in range(2):
            acc[kk] += product(1, kk, 2)
        factor_ready(3)
        arrived(y_in.at[2], Y_IN + 2)
        for kk in range(2):
            put_p(1, kk, acc[kk] + product(2, kk, 3))
        to_owner(1, 5)

        @pl.when(own)
        def _():
            solve_forward(1)
            solve_back(1)
            to_line(1, 6)

        arrived(x_in.at[1], X_IN + 1)
        for line in range(4):
            put_q(0, line, back_product(1, 3, line))
        to_supernode(0, 2, 0, 9)

        @pl.when(own)
        def _():
            to_plane(y_own.at[1], 1, 8, Y_ALL + 1)
            to_plane(x_own.at[1], 3, 7, X_ALL + 1)

        for line in range(4):
            put_q(1, line, back_product(1, 2, line))
        for line in range(4):
            q_acc[line] = back_product(1, 1, line)
        write_y(1)
        to_supernode(1, 0, 1, 10)
        write_x(1)

        @pl.when(own)
        def _():
            solve_back(0, 0, 1)
            to_line(0, 11)

        arrived(x_in.at[0], X_IN)
        for line in range(4):
            put_q(2, line, q_acc[line] + back_product(0, 0, line))
        to_supernode(2, 1, 0, 13)

        @pl.when(own)
        def _():
            to_plane(x_own.at[0], 2, 12, X_ALL)

        write_x(0)
        for index in range(4):
            factor_sent(index)
        sent_unless(own, 1, 2)
        sent_unless(own, 5, 2)
        sent(9, 4)
        sent_unless(own, 10, 4)
        sent(13, 4)

        @pl.when(source)
        def _():
            for core in range(2):
                share(core, False)

        @pl.when(own)
        def _():
            sent(3, 7)
            sent_unless(source, 4, 16)
            sent(6, 3)
            sent_unless(source, 7, 16)
            sent_unless(source, 8, 16)
            sent(11, 3)
            sent_unless(source, 12, 16)


def per_device(factor, pattern, dinv, rhs):
    bf16, f32 = jnp.bfloat16, jnp.float32
    vmem = pl.BlockSpec(memory_space=pltpu.VMEM)
    result = pl.pallas_call(
        kernel,
        out_shape=jax.ShapeDtypeStruct((2, 2, 256, 256), bf16),
        in_specs=[pl.BlockSpec(memory_space=pltpu.HBM)] * 4,
        out_specs=vmem,
        scratch_shapes=[
            pltpu.SMEM((2, 4), jnp.int32),
            pltpu.VMEM((4, 256, 256), bf16),
            pltpu.VMEM((2, 256, 256), bf16),
            pltpu.VMEM((2, 256, 256), f32),
            pltpu.VMEM((2, 4, 4, 256, 256), bf16),
            pltpu.VMEM((2, 256, 256), bf16),
            pltpu.VMEM((2, 2, 32, 256), f32),
            pltpu.VMEM((2, 32, 256), f32),
            pltpu.VMEM((2, 32, 256), bf16),
            pltpu.VMEM((2, 32, 256), bf16),
            pltpu.VMEM((2, 32, 256), bf16),
            pltpu.VMEM((3, 4, 32, 256), bf16),
            pltpu.VMEM((2, 2, 32, 256), bf16),
            pltpu.VMEM((2, 4, 32, 256), bf16),
            pltpu.VMEM((2, 32, 256), f32),
            pltpu.VMEM((32, 32, 256), bf16),
            pltpu.VMEM((2, 2, 32, 256), bf16),
            pltpu.VMEM((256, 256), f32),
            pltpu.VMEM((4, 32, 256), f32),
            pltpu.VMEM((3, 4, 32, 256), bf16),
            pltpu.VMEM((3, 8, 32, 256), bf16),
            pltpu.SemaphoreType.DMA((24,)),
            pltpu.SemaphoreType.DMA((25,)),
            pltpu.SemaphoreType.DMA((7,)),
        ],
        compiler_params=pltpu.CompilerParams(
            collective_id=0, has_side_effects=True, vmem_limit_bytes=60 * 1024 * 1024
        ),
        cost_estimate=pl.CostEstimate(flops=600_000_000, bytes_accessed=3_000_000, transcendentals=0),
    )(pattern[:, 0, :, 0], factor[:, 0, :, 0], dinv[:, 0], rhs[:, 0])
    return result[0][:, None], result[1][:, None]


def solution(mesh):
    placed = (
        P(None, "row", None, "col", None, None),
        P(None, "row", None, "col"),
        P(None, "row", None, None),
        P(None, "row", None, None),
    )
    return jax.shard_map(
        per_device,
        mesh=mesh,
        in_specs=placed,
        out_specs=(P(None, "row", None, None), P(None, "row", None, None)),
        check_vma=False,
    )
```

time: 108 us -> 105 us (0.972)
  Pallas kernels: 104 us -> 102 us
    pallas_call x1, Pallas kernels: 104 us -> 102 us  [per_device(): pl.pallas_call(kernel, out_shape=jax.ShapeDtypeStruct((2, 2, 256, 256), b...]
    unnamed x4 -> x1, local copies, waits for them, and re-layouts: 2.42 us -> 1.85 us
where the time goes in v3:
time: 105 us
  Pallas kernels  102 us (97%)
  local copies, waits for them, and re-layouts  1.85 us (2%)
    pallas_call x1, Pallas kernels, per_device(): pl.pallas_call(kernel, out_shape=jax.ShapeDtypeStruct((2, 2, 256, 256), b...  102 us

profile of v3, /device:TPU:1, one launch (start us, length us, event | category | flops | bytes accessed | tf_op | source)
XLA Modules:
  0.0 104.7 jit_solution(9038163947640148232)
XLA Ops:
  0.6 102.2 %shard_map.59 = bf16[2,2,256,256]{3,2,1,0:T(8,128)(2,1)} custom-call(s32[2,4]{1,0:T(2,128)} %bitcast.15, bf16[2,4,256,256]{3,2,1,0:T(8,128)(2,1)} %bitcast.12, bf16[2,256,256]{2,1,0:T(8,128)(2,1)} %bitcast.14, f32[2,256,256]{2,1,0:T(8,128)} %bitcast.13), custom_call_target="tpu_custom_call" | custom-call | flops 600000000 | bytes 3000000 | tf_op jit(solution)/shard_map/pallas_call | solution.py:461
  102.8 1.9 %slice_bitcast_fusion = (bf16[2,1,256,256]{3,2,1,0:T(8,128)(2,1)}, bf16[2,1,256,256]{3,2,1,0:T(8,128)(2,1)}) fusion(bf16[2,2,256,256]{3,2,1,0:T(8,128)(2,1)} %shard_map.59), kind=kLoop, calls=%fused_computation | loop fusion | bytes 1048576

commit v4 on v3

--- a/solution.py
+++ b/solution.py
@@ -143,6 +143,16 @@
         def _(p):
             remote(src, dst, event, cls, row, (c + p) % 16).start()
 
+    def to_lines(slot, event):
+        for p in range(4):
+            for core in range(2):
+                args = (x_in.at[slot, core], full.at[16 + 8 * slot + 2 * x + k], event, X_ALL + slot,
+                        2 * z + core, 4 * ((x + p) % 4) + y)
+                if p == 0:
+                    send(*args, core == k)
+                else:
+                    remote(*args).start()
+
     def to_supernode(slot, cls, half, event):
         for p in range(4):
             line = (line_own + p) % 4
@@ -267,17 +277,13 @@
             for core in range(2):
                 share(core, True)
                 send(y_0.at[core], y_own.at[0], 0, Y0_IN, 2 * z + core, c, core == k)
+            sent(1, 16)
+            first_to_column(0, 2)
 
         gather(1)
         gather(2)
         out[0, 0] = exact_dot(rhs[0].T, dinv[0], NT).T.astype(jnp.bfloat16)
         gathered(1)
-
-        @pl.when(source)
-        def _():
-            sent(1, 16)
-            first_to_column(0, 2)
-
         gathered(2)
         factor_ready(1)
         arrived(y_in.at[0], Y_IN)
@@ -312,10 +318,7 @@
         for line in range(4):
             put_q(1, line, back_product(1, 1, line))
 
-        @pl.when(own)
-        def _():
-            to_plane(x_own.at[1], 3, 7, X_ALL + 1)
-
+        to_lines(1, 7)
         to_supernode(1, 0, 0, 9)
         write_x(1)
 
@@ -329,6 +332,7 @@
             factor_sent(index)
         sent_unless(own, 3, 2)
         sent(8, 4)
+        sent(7, 7)
         sent_unless(own, 9, 4)
 
         @pl.when(source)
@@ -342,7 +346,6 @@
         def _():
             sent_unless(source, 5, 16)
             sent(6, 3)
-            sent_unless(source, 7, 16)
             sent_unless(source, 10, 16)
 
     @pl.when(h == 1)
@@ -369,23 +372,23 @@
             solve_forward(0)
             to_column(0, 1, 0, 2)
             sent(2, 8)
-            to_plane(y_own.at[0], 0, 4, Y_ALL)
+            to_column(0, 1, 1, 3)
 
         for index in range(1, 4):
             gathered(index)
         factor_ready(1)
         for kk in range(2):
             acc[kk] = product(0, kk, 1)
-        write_y(0)
-
-        @pl.when(own)
-        def _():
-            to_column(0, 1, 1, 3)
+
+        @pl.when(own)
+        def _():
+            to_plane(y_own.at[0], 0, 4, Y_ALL)
 
         factor_ready(2)
         arrived(y_in.at[1], Y_IN + 1)
         for kk in range(2):
             acc[kk] += product(1, kk, 2)
+        write_y(0)
         factor_ready(3)
         arrived(y_in.at[2], Y_IN + 2)
         for kk in range(2):
@@ -402,11 +405,11 @@
         for line in range(4):
             put_q(0, line, back_product(1, 3, line))
         to_supernode(0, 2, 0, 9)
+        to_lines(1, 7)
 
         @pl.when(own)
         def _():
             to_plane(y_own.at[1], 1, 8, Y_ALL + 1)
-            to_plane(x_own.at[1], 3, 7, X_ALL + 1)
 
         for line in range(4):
             put_q(1, line, back_product(1, 2, line))
@@ -426,16 +429,15 @@
             put_q(2, line, q_acc[line] + back_product(0, 0, line))
         to_supernode(2, 1, 0, 13)
 
-        @pl.when(own)
-        def _():
-            to_plane(x_own.at[0], 2, 12, X_ALL)
-
+        to_lines(0, 12)
         write_x(0)
         for index in range(4):
             factor_sent(index)
         sent_unless(own, 1, 2)
         sent_unless(own, 5, 2)
         sent(9, 4)
+        sent(7, 7)
+        sent(12, 7)
         sent_unless(own, 10, 4)
         sent(13, 4)
 
@@ -449,10 +451,8 @@
             sent(3, 7)
             sent_unless(source, 4, 16)
             sent(6, 3)
-            sent_unless(source, 7, 16)
             sent_unless(source, 8, 16)
             sent(11, 3)
-            sent_unless(source, 12, 16)
 
 
 def per_device(factor, pattern, dinv, rhs):

time: 105 us -> 102 us (0.971)
  Pallas kernels: 102 us -> 99.7 us
    pallas_call x1, Pallas kernels: 102 us -> 99.7 us  [per_device(): pl.pallas_call(kernel, out_shape=jax.ShapeDtypeStruct((2, 2, 256, 256), b...]
where the time goes in v4:
time: 102 us
  Pallas kernels  99.7 us (98%)
  local copies, waits for them, and re-layouts  1.85 us (2%)
    pallas_call x1, Pallas kernels, per_device(): pl.pallas_call(kernel, out_shape=jax.ShapeDtypeStruct((2, 2, 256, 256), b...  99.7 us

profile of v4, /device:TPU:1, one launch (start us, length us, event | category | flops | bytes accessed | tf_op | source)
XLA Modules:
  0.0 102.2 jit_solution(10498702636818504674)
XLA Ops:
  0.6 99.7 %shard_map.59 = bf16[2,2,256,256]{3,2,1,0:T(8,128)(2,1)} custom-call(s32[2,4]{1,0:T(2,128)} %bitcast.15, bf16[2,4,256,256]{3,2,1,0:T(8,128)(2,1)} %bitcast.12, bf16[2,256,256]{2,1,0:T(8,128)(2,1)} %bitcast.14, f32[2,256,256]{2,1,0:T(8,128)} %bitcast.13), custom_call_target="tpu_custom_call" | custom-call | flops 600000000 | bytes 3000000 | tf_op jit(solution)/shard_map/pallas_call | solution.py:461
  100.3 1.9 %slice_bitcast_fusion = (bf16[2,1,256,256]{3,2,1,0:T(8,128)(2,1)}, bf16[2,1,256,256]{3,2,1,0:T(8,128)(2,1)}) fusion(bf16[2,2,256,256]{3,2,1,0:T(8,128)(2,1)} %shard_map.59), kind=kLoop, calls=%fused_computation | loop fusion | bytes 1048576

commit v5 on v4

--- a/solution.py
+++ b/solution.py
@@ -9,7 +9,7 @@
 NT = (((1,), (1,)), ((), ()))
 NN = (((1,), (0,)), ((), ()))
 PLACES = ((0, 0), (1, 0), (1, 1), (1, 2))
-Y_IN, P_IN, Y_ALL, X_IN, X_ALL, Q_IN, L_IN, G_IN, D_IN, B_IN, Y0_IN = 0, 3, 5, 7, 9, 11, 14, 18, 22, 23, 24
+Y_IN, P_IN, Y_ALL, X_IN, X_ALL, Q_IN, L_IN, G_IN, D_IN, B_IN, Y0_IN, G_0 = 0, 3, 5, 7, 9, 11, 14, 18, 22, 23, 24, 25
 
 
 def exact_dot(lhs, inverse, dims):
@@ -172,16 +172,24 @@
                 pl.when(core != k)(remote(src, dst, 22 + i, cls, 2 * z + core, c).wait_send)
 
     def gather(index):
-        for p in range(1, 4):
-            block = blocks.at[k, index, x]
-            remote(block, block, 14 + index, G_IN + index, r, 4 * ((x + p) % 4) + y).start()
-
-    def swap(index):
-        return remote(blocks.at[k, index], blocks.at[k, index], 18 + index, L_IN + index, 2 * z + 1 - k, c)
+        block = blocks.at[k, index, x]
+        for p in (2, 1, 3):
+            cls = G_0 + p - 1 if index == 0 else G_IN + index
+            remote(block, block, 14 + index, cls, r, 4 * ((x + p) % 4) + y).start()
+        swap(index, x).start()
+
+    def swap(index, line):
+        block = blocks.at[k, index, line]
+        return remote(block, block, 18 + index, L_IN + index, 2 * z + 1 - k, c)
 
     def gathered(index):
-        arrived(blocks.at[k, index, pl.ds(0, 3)], G_IN + index)
-        swap(index).start()
+        if index > 0:
+            arrived(blocks.at[k, index, pl.ds(0, 3)], G_IN + index)
+        for p in (1, 3, 2):
+            line = (x + 4 - p) % 4
+            if index == 0:
+                arrived(blocks.at[k, index, line], G_0 + p - 1)
+            swap(index, line).start()
 
     def factor_ready(index):
         arrived(blocks.at[1 - k, index], L_IN + index)
@@ -189,7 +197,8 @@
     def factor_sent(index):
         d = blocks.at[k, index, pl.ds(0, 3)]
         remote(d, d, 14 + index, 0, r, c).wait_send()
-        swap(index).wait_send()
+        d = blocks.at[k, index]
+        remote(d, d, 18 + index, 0, r, c).wait_send()
 
     def product(level, kk, index):
         total = None
@@ -486,7 +495,7 @@
             pltpu.VMEM((3, 4, 32, 256), bf16),
             pltpu.VMEM((3, 8, 32, 256), bf16),
             pltpu.SemaphoreType.DMA((24,)),
-            pltpu.SemaphoreType.DMA((25,)),
+            pltpu.SemaphoreType.DMA((28,)),
             pltpu.SemaphoreType.DMA((7,)),
         ],
         compiler_params=pltpu.CompilerParams(

time: 102 us -> 102 us (level)
  no operation moved by 1% of the time
where the time goes in v5:
time: 102 us; the launch traced here: 101 us
  Pallas kernels  98.9 us (97%)
  local copies, waits for them, and re-layouts  1.85 us (2%)
    pallas_call x1, Pallas kernels, per_device(): pl.pallas_call(kernel, out_shape=jax.ShapeDtypeStruct((2, 2, 256, 256), b...  98.9 us

profile of v5, /device:TPU:1, one launch (start us, length us, event | category | flops | bytes accessed | tf_op | source)
XLA Modules:
  0.0 101.4 jit_solution(12330388860932369428)
XLA Ops:
  0.6 98.9 %shard_map.59 = bf16[2,2,256,256]{3,2,1,0:T(8,128)(2,1)} custom-call(s32[2,4]{1,0:T(2,128)} %bitcast.15, bf16[2,4,256,256]{3,2,1,0:T(8,128)(2,1)} %bitcast.12, bf16[2,256,256]{2,1,0:T(8,128)(2,1)} %bitcast.14, f32[2,256,256]{2,1,0:T(8,128)} %bitcast.13), custom_call_target="tpu_custom_call" | custom-call | flops 600000000 | bytes 3000000 | tf_op jit(solution)/shard_map/pallas_call | solution.py:470
  99.5 1.9 %slice_bitcast_fusion = (bf16[2,1,256,256]{3,2,1,0:T(8,128)(2,1)}, bf16[2,1,256,256]{3,2,1,0:T(8,128)(2,1)}) fusion(bf16[2,2,256,256]{3,2,1,0:T(8,128)(2,1)} %shard_map.59), kind=kLoop, calls=%fused_computation | loop fusion | bytes 1048576

commit v6 on v5

--- a/solution.py
+++ b/solution.py
@@ -367,13 +367,13 @@
                 share(core, True)
 
         gathered(0)
+        factor_ready(0)
+        arrived(y_in.at[0], Y_IN)
+        for kk in range(2):
+            put_p(0, kk, product(0, kk, 0))
+        to_owner(0, 1)
         for index in range(1, 4):
             gather(index)
-        factor_ready(0)
-        arrived(y_in.at[0], Y_IN)
-        for kk in range(2):
-            put_p(0, kk, product(0, kk, 0))
-        to_owner(0, 1)
 
         @pl.when(own)
         def _():

time: 102 us -> 102 us (level)
  no operation moved by 1% of the time
where the time goes in v6:
time: 102 us; the launch traced here: 101 us
  Pallas kernels  98.9 us (97%)
  local copies, waits for them, and re-layouts  1.85 us (2%)
    pallas_call x1, Pallas kernels, per_device(): pl.pallas_call(kernel, out_shape=jax.ShapeDtypeStruct((2, 2, 256, 256), b...  98.9 us

profile of v6, /device:TPU:1, one launch (start us, length us, event | category | flops | bytes accessed | tf_op | source)
XLA Modules:
  0.0 101.4 jit_solution(16275749843475970931)
XLA Ops:
  0.6 98.9 %shard_map.59 = bf16[2,2,256,256]{3,2,1,0:T(8,128)(2,1)} custom-call(s32[2,4]{1,0:T(2,128)} %bitcast.15, bf16[2,4,256,256]{3,2,1,0:T(8,128)(2,1)} %bitcast.12, bf16[2,256,256]{2,1,0:T(8,128)(2,1)} %bitcast.14, f32[2,256,256]{2,1,0:T(8,128)} %bitcast.13), custom_call_target="tpu_custom_call" | custom-call | flops 600000000 | bytes 3000000 | tf_op jit(solution)/shard_map/pallas_call | solution.py:470
  99.6 1.9 %slice_bitcast_fusion = (bf16[2,1,256,256]{3,2,1,0:T(8,128)(2,1)}, bf16[2,1,256,256]{3,2,1,0:T(8,128)(2,1)}) fusion(bf16[2,2,256,256]{3,2,1,0:T(8,128)(2,1)} %shard_map.59), kind=kLoop, calls=%fused_computation | loop fusion | bytes 1048576
